TPU v7x, 32 devices: a whole 2x2x4 slice. The times are simulated.
32 devices in a mesh: section: 2 (over core), expert: 16 (over z, y, x).
Axes of the slice: x: 2, y: 2, z: 4, core: 2. Of those that a mesh axis runs over, the one named last changes fastest.
Arguments:
- grad_out: bfloat16 [2, 2048, 3584], P('section', 'expert'), may hold values from -6 to 6
- expert_ids: int32 [2, 2048, 8], P('section', 'expert'), may hold values from 0 to 15, all different within a row; in each aligned block of 128 rows (0 to 127, 128 to 255, ..., all dimensions but the last counted through in order) at most 80 rows name the same one
- gate_weights: bfloat16 [2, 2048, 8], P('section', 'expert'), may hold values from 0.019897461 to 0.5
- down_weight: bfloat16 [2, 16, 1024, 3584], P('section', 'expert'), may hold values from -0.09375 to 0.09375
- hidden_saved: bfloat16 [2, 16, 16, 80, 1024], P('section', 'expert'), may hold values from -0.19921875 to 0.19921875
Outputs:
- hidden_grad: bfloat16 [2, 16, 16, 80, 1024], P('section', 'expert')
- gate_grad: float32 [2, 2048, 8], P('section', 'expert')
Inputs may be any that keep to these rules, and one draw needn't show every extreme that they name: `expert_ids`: each token names 8 distinct experts; among the tokens of one index of expert in one section, no expert is named by more than 80 of them, a bound that some block reaches.
All inputs are finite; a program needn't handle non-finite values.
Results may differ from a plain program's by a relative error of at most 0.001.
Values may be sent and summed in bfloat16 or wider, within the bound.
A program may use at most 128 MiB of HBM per device.

v0:
```python
import jax
import jax.numpy as jnp
from jax import lax
from jax.sharding import PartitionSpec as P


def shifted(x, axis, by):
    size = lax.axis_size(axis)
    return lax.ppermute(x, axis, [(i, (i + by) % size) for i in range(size)])


def slot_places(ids_local, experts, most):
    flat = ids_local.reshape(-1)
    onehot = (flat[:, None] == jnp.arange(experts, dtype=jnp.int32)[None, :]).astype(jnp.int32)
    rank = jnp.sum(jnp.cumsum(onehot, 0) * onehot, 1) - 1
    return flat * most + rank


def pack_rows(grad_local, dest, experts, most, top_count):
    token = jnp.arange(dest.shape[0], dtype=jnp.int32) // top_count
    rows = (
        jnp.zeros((experts * most, grad_local.shape[1]), jnp.bfloat16)
        .at[dest]
        .set(grad_local[token])
    )
    return rows.reshape(experts, most, grad_local.shape[1])


def pack_gates(gates_local, dest, experts, most):
    weights = jnp.zeros((experts * most,), jnp.bfloat16).at[dest].set(gates_local.reshape(-1))
    return weights.reshape(experts, most)


def project_back(rows_in, weight_part):
    flat_rows = rows_in.reshape(-1, rows_in.shape[2])
    return lax.dot_general(
        flat_rows, weight_part, (((1,), (1,)), ((), ())), preferred_element_type=jnp.float32
    )


def local(grad_out, expert_ids, gate_weights, down_weight, hidden_saved):
    experts = lax.axis_size("expert")
    most = hidden_saved.shape[3]
    width = grad_out.shape[2]
    hidden_width = down_weight.shape[2]
    top_count = expert_ids.shape[2]
    dest = slot_places(expert_ids[0], experts, most)
    gate_buf = pack_gates(gate_weights[0], dest, experts, most)
    half = width // 2
    lower = shifted(grad_out[0][:, :half], "section", -1)
    lower_buf = pack_rows(lower, dest, experts, most, top_count)
    lower_in, gates_in = (
        lax.all_to_all(lower_buf, "expert", split_axis=0, concat_axis=0, tiled=True),
        lax.all_to_all(gate_buf, "expert", split_axis=0, concat_axis=0, tiled=True),
    )
    upper = shifted(grad_out[0][:, half:], "section", -1)
    upper_buf = pack_rows(upper, dest, experts, most, top_count)
    upper_in = lax.all_to_all(upper_buf, "expert", split_axis=0, concat_axis=0, tiled=True)
    back = project_back(lower_in, down_weight[0, 0][:, :half]) + project_back(
        upper_in, down_weight[0, 0][:, half:]
    )
    hidden_grad = (gates_in.reshape(-1).astype(jnp.float32)[:, None] * back).astype(jnp.bfloat16)
    saved = hidden_saved[0, 0].reshape(experts * most, hidden_width)
    slot_grad = jnp.sum(saved.astype(jnp.float32) * back, axis=1).reshape(experts, most)
    returned = lax.all_to_all(slot_grad, "expert", split_axis=0, concat_axis=0, tiled=True)
    gate_grad = returned.reshape(-1)[dest].reshape(1, expert_ids.shape[1], top_count)
    return (hidden_grad.reshape(1, 1, experts, most, hidden_width), gate_grad)


def solution(mesh):
    in_specs = (
        P("section", "expert", None),
        P("section", "expert", None),
        P("section", "expert", None),
        P("section", "expert", None, None),
        P("section", "expert", None, None, None),
    )
    out_specs = (P("section", "expert", None, None, None), P("section", "expert", None))
    return jax.shard_map(local, mesh=mesh, in_specs=in_specs, out_specs=out_specs, check_vma=False)
```

profile of v0, /device:TPU:0, one launch (start us, length us, event | category | flops | bytes accessed | tf_op | source)
XLA Modules:
  0.0 297.8 jit_solution(12047823034583232656)
XLA Ops:
  0.6 1.2 fusion.15
  1.9 0.5 collective-permute-start
  2.4 0.8 copy.17
  3.2 0.1 eq.29
  3.2 0.1 eq.25
  3.3 0.7 broadcast_multiply_fusion
  4.0 4.5 %reduce-window.6 = s32[16,8,128]{2,1,0:T(8,128)S(1)} reduce-window(s32[16,8,128]{2,1,0:T(8,128)S(1)} %fusion.12, s32[]{:T(128)} %constant.31.clone.1), window={size=1x1x128 pad=0_0x0_0x127_0}, to_apply=%region_0.0 | reduce-window | flops 2080768 | bytes 131076 | tf_op jit(solution)/shard_map/reduce-window
  8.6 0.1 slice.30
  8.6 0.1 copy.19
  8.8 0.1 copy.20
  8.9 0.1 broadcast_add_fusion
  9.0 0.1 copy.16
  9.1 0.1 mul.32
  9.2 0.8 copy.21
  10.0 0.1 reshape.176
  10.1 7.6 %scatter_custom_fusion = bf16[1280]{0:T(1024)(128)(2,1)S(1)} fusion(s32[1024]{0:T(1024)S(1)} %bitcast.34, bf16[1024]{0:T(1024)(128)(2,1)S(1)} %reshape.176, bf16[]{:T(256)} %constant.29.clone.1), kind=kCustom, calls=%fused_computation.37 | custom fusion | bytes 2562 | tf_op jit(solution)/shard_map/scatter | solution.py:30
  17.7 0.7 all_to_all.24
  18.4 8.3 %all-to-all-start = ((bf16[16,1,80]{2,1,0:T(2,128)(2,1)}), bf16[16,1,80]{2,1,0:T(2,128)(2,1)S(1)}, u32[]{:S(2)}, u32[]{:S(2)}) async-start(bf16[16,1,80]{2,1,0:T(2,128)(2,1)} %all_to_all.24), calls=%async_computation | async-start | bytes 16384 | tf_op jit(solution)/shard_map/all_to_all | solution.py:54
  26.8 0.0 collective-permute-done
  26.8 20.6 %scatter_custom_fusion.1 = bf16[1280,1792]{1,0:T(8,128)(2,1)} fusion(s32[1024]{0:T(1024)S(1)} %bitcast.35, bf16[128,1792]{1,0:T(8,128)(2,1)S(1)} %collective-permute-done, s32[1024]{0:T(1024)S(1)} %broadcast_clamp_fusion.1, bf16[]{:T(256)} %constant.29.clone.1), kind=kCustom, calls=%fused_computation.15 | custom fusion | bytes 4587522 | tf_op jit(solution)/shard_map/scatter | solution.py:24
  47.4 0.0 all-to-all-done
  47.4 7.2 %all-to-all-start.1 = ((bf16[16,80,1792]{2,1,0:T(8,128)(2,1)}), bf16[16,80,1792]{2,1,0:T(8,128)(2,1)}, u32[]{:S(2)}, u32[]{:S(2)}) async-start(bf16[16,80,1792]{2,1,0:T(8,128)(2,1)} %bitcast.29), calls=%async_computation.1 | async-start | bytes 9175040 | tf_op jit(solution)/shard_map/all_to_all | solution.py:53
  54.6 0.1 collective-permute-start.1
  54.7 1.8 collective-permute-done.1
  56.5 20.7 %scatter_custom_fusion.2 = bf16[1280,1792]{1,0:T(8,128)(2,1)} fusion(s32[1024]{0:T(1024)S(1)} %bitcast.36, bf16[128,1792]{1,0:T(8,128)(2,1)S(1)} %collective-permute-done.1, s32[1024]{0:T(1024)S(1)} %broadcast_clamp_fusion.1, bf16[]{:T(256)} %constant.29.clone.1), kind=kCustom, calls=%fused_computation.13 | custom fusion | bytes 4587522 | tf_op jit(solution)/shard_map/scatter | solution.py:24
  77.2 64.5 %all-to-all-done.1 = bf16[16,80,1792]{2,1,0:T(8,128)(2,1)} async-done(((bf16[16,80,1792]{2,1,0:T(8,128)(2,1)}), bf16[16,80,1792]{2,1,0:T(8,128)(2,1)}, u32[]{:S(2)}, u32[]{:S(2)}) %all-to-all-start.1) | async-done | bytes 4587552 | tf_op jit(solution)/shard_map/all_to_all | solution.py:53
  141.7 22.0 %all-to-all-start.2 = ((bf16[16,80,1792]{2,1,0:T(8,128)(2,1)}), bf16[16,80,1792]{2,1,0:T(8,128)(2,1)}, u32[]{:S(2)}, u32[]{:S(2)}) async-start(bf16[16,80,1792]{2,1,0:T(8,128)(2,1)} %bitcast.30), calls=%async_computation.2 | async-start | bytes 9175040 | tf_op jit(solution)/shard_map/all_to_all | solution.py:58
  163.7 0.1 reshape.146
  163.8 0.0 copy-start
  163.8 10.8 %fusion.2 = f32[1280,1024]{1,0:T(8,128)} fusion(bf16[1280,1792]{1,0:T(8,128)(2,1)} %bitcast.7, bf16[1024,3584]{1,0:T(8,128)(2,1)} %bitcast.40), kind=kOutput, calls=%fused_computation.11 | convolution fusion | flops 4697620480 | bytes 13500416 | tf_op jit(solution)/shard_map/dot_general | solution.py:36
  174.6 74.2 %all-to-all-done.2 = bf16[16,80,1792]{2,1,0:T(8,128)(2,1)} async-done(((bf16[16,80,1792]{2,1,0:T(8,128)(2,1)}), bf16[16,80,1792]{2,1,0:T(8,128)(2,1)}, u32[]{:S(2)}, u32[]{:S(2)}) %all-to-all-start.2) | async-done | bytes 4587552 | tf_op jit(solution)/shard_map/all_to_all | solution.py:58
  248.8 0.0 copy-done
  248.8 11.7 %fusion = (f32[1280]{0:T(1024)S(1)}, bf16[1280,1024]{1,0:T(8,128)(2,1)}) fusion(bf16[1,1,16,80,1024]{4,3,2,1,0:T(8,128)(2,1)S(1)} %copy-done, f32[1280]{0:T(1024)S(1)} %reshape.146, f32[1280,1024]{1,0:T(8,128)} %fusion.2, bf16[1280,1792]{1,0:T(8,128)(2,1)} %bitcast.10, bf16[1024,3584]{1,0:T(8,128)(2,1)} %bitcast.41), kind=kOutput, calls=%fused_computation.7 | convolution fusion | flops 4705483776 | bytes 18753536 | tf_op jit(solution)/shard_map/dot_general | solution.py:36
  260.5 0.7 all_to_all.22
  261.2 21.0 %all-to-all-start.3 = ((f32[16,1,80]{2,1,0:T(1,128)}), f32[16,1,80]{2,1,0:T(1,128)S(1)}, u32[]{:S(2)}, u32[]{:S(2)}) async-start(f32[16,1,80]{2,1,0:T(1,128)} %all_to_all.22), calls=%async_computation.3 | async-start | bytes 16384 | tf_op jit(solution)/shard_map/all_to_all | solution.py:65
  282.2 7.3 %all-to-all-done.3 = f32[16,1,80]{2,1,0:T(1,128)S(1)} async-done(((f32[16,1,80]{2,1,0:T(1,128)}), f32[16,1,80]{2,1,0:T(1,128)S(1)}, u32[]{:S(2)}, u32[]{:S(2)}) %all-to-all-start.3) | async-done | bytes 5152 | tf_op jit(solution)/shard_map/all_to_all | solution.py:65
  289.4 0.5 broadcast.157
  290.0 0.7 reduce.7
  290.6 0.1 reshape.144
  290.7 6.1 %gather_fusion = f32[1024]{0:T(1024)S(1)} fusion(f32[1280]{0:T(1024)S(1)} %reshape.144, s32[1024]{0:T(1024)S(1)} %broadcast_clamp_fusion), kind=kCustom, calls=%fused_computation.2 | custom fusion | bytes 12288 | tf_op jit(solution)/shard_map/gather | solution.py:66
  296.9 0.1 reshape.145
  296.9 0.7 copy.23
  (10 shorter events, 0.1 us)
Async XLA Ops:
  1.9 25.0 %collective-permute-start = (bf16[128,1792]{1,0:T(8,128)(2,1)S(1)}, bf16[128,1792]{1,0:T(8,128)(2,1)S(1)}, u32[]{:S(2)}, u32[]{:S(2)}) collective-permute-start(bf16[128,1792]{1,0:T(8,128)(2,1)S(1)} %get-tuple-element.9), channel_id=1, source_target_pairs={{0,16},{16,0},{1,17},{17,1},{2,18},{18,2},{3,19},{19,3},{4,20},{20... | collective-permute-start | bytes 1376264 | tf_op jit(solution)/shard_map/ppermute | solution.py:9
  18.4 28.9 %all-to-all-start = ((bf16[16,1,80]{2,1,0:T(2,128)(2,1)}), bf16[16,1,80]{2,1,0:T(2,128)(2,1)S(1)}, u32[]{:S(2)}, u32[]{:S(2)}) async-start(bf16[16,1,80]{2,1,0:T(2,128)(2,1)} %all_to_all.24), calls=%async_computation | async-start | bytes 16384 | tf_op jit(solution)/shard_map/all_to_all | solution.py:54
  47.4 94.3 %all-to-all-start.1 = ((bf16[16,80,1792]{2,1,0:T(8,128)(2,1)}), bf16[16,80,1792]{2,1,0:T(8,128)(2,1)}, u32[]{:S(2)}, u32[]{:S(2)}) async-start(bf16[16,80,1792]{2,1,0:T(8,128)(2,1)} %bitcast.29), calls=%async_computation.1 | async-start | bytes 9175040 | tf_op jit(solution)/shard_map/all_to_all | solution.py:53
  54.6 1.9 collective-permute-start.1
  141.7 107.1 %all-to-all-start.2 = ((bf16[16,80,1792]{2,1,0:T(8,128)(2,1)}), bf16[16,80,1792]{2,1,0:T(8,128)(2,1)}, u32[]{:S(2)}, u32[]{:S(2)}) async-start(bf16[16,80,1792]{2,1,0:T(8,128)(2,1)} %bitcast.30), calls=%async_computation.2 | async-start | bytes 9175040 | tf_op jit(solution)/shard_map/all_to_all | solution.py:58
  163.8 85.1 %copy-start = (bf16[1,1,16,80,1024]{4,3,2,1,0:T(8,128)(2,1)S(1)}, bf16[1,1,16,80,1024]{4,3,2,1,0:T(8,128)(2,1)}, u32[]{:S(2)}) copy-start(bf16[1,1,16,80,1024]{4,3,2,1,0:T(8,128)(2,1)} %param.9) | copy-start | bytes 7864324
  261.2 28.2 %all-to-all-start.3 = ((f32[16,1,80]{2,1,0:T(1,128)}), f32[16,1,80]{2,1,0:T(1,128)S(1)}, u32[]{:S(2)}, u32[]{:S(2)}) async-start(f32[16,1,80]{2,1,0:T(1,128)} %all_to_all.22), calls=%async_computation.3 | async-start | bytes 16384 | tf_op jit(solution)/shard_map/all_to_all | solution.py:65
where the time goes:
time: 302 us; the launch traced here: 298 us
  waiting for transfers between devices  148 us (49%)
  local copies, waits for them, and re-layouts  61.3 us (20%)
  starting transfers between devices  59.1 us (20%)
  matrix products  22.5 us (7%)
  other arithmetic  6.09 us (2%)
    all_to_all x1, waiting for transfers between devices, local(): lax.all_to_all(upper_buf, 'expert', split_axis=0, concat_axis=0, tiled=True)  74.2 us
    all_to_all x1, waiting for transfers between devices, local(): lax.all_to_all(lower_buf, 'expert', split_axis=0, concat_axis=0, tiled=True)  64.5 us
    scatter x2, local copies, waits for them, and re-layouts, pack_rows(): rows = jnp.zeros((experts * most, grad_local.shape[1]), jnp.bfloat16).at[...  41.2 us
    dot_general x2, matrix products, project_back(): lax.dot_general(flat_rows, weight_part, (((1,), (1,)), ((), ())), preferr...  22.5 us
    all_to_all x1, starting transfers between devices, local(): lax.all_to_all(upper_buf, 'expert', split_axis=0, concat_axis=0, tiled=True)  22 us
    all_to_all x1, starting transfers between devices, local(): lax.all_to_all(slot_grad, 'expert', split_axis=0, concat_axis=0, tiled=True)  21 us
    all_to_all x1, starting transfers between devices, local(): lax.all_to_all(gate_buf, 'expert', split_axis=0, concat_axis=0, tiled=True)  8.34 us
    scatter x1, local copies, waits for them, and re-layouts, pack_gates(): jnp.zeros((experts * most,), jnp.bfloat16).at[dest]  7.59 us
  transfers between devices with their start and end apart: 6, of which 4 were waited for; matrix products, arithmetic and copies ran while one was open for 23% of the time, Pallas kernels for 0%

commit v1 on v0

--- a/solution.py
+++ b/solution.py
@@ -67,6 +67,39 @@
     return (hidden_grad.reshape(1, 1, experts, most, hidden_width), gate_grad)
 
 
+def gathered(grad_out, expert_ids, gate_weights, down_weight, hidden_saved):
+    experts = lax.axis_size("expert")
+    most = hidden_saved.shape[3]
+    width = grad_out.shape[2]
+    tokens = grad_out.shape[1]
+    hidden_width = down_weight.shape[2]
+    me = lax.axis_index("expert")
+    ids = lax.all_gather(expert_ids[0], "expert", axis=0)
+    gates = lax.all_gather(gate_weights[0], "expert", axis=0)
+    incoming = shifted(grad_out[0], "section", -1)
+    grads = lax.all_gather(incoming, "expert", axis=0)
+    named = ids == me
+    owned = jnp.any(named, axis=2)
+    place = jnp.arange(tokens, dtype=jnp.int32)
+    earlier = (place[:, None] < place[None, :]).astype(jnp.bfloat16)
+    before = jnp.dot(owned.astype(jnp.bfloat16), earlier, preferred_element_type=jnp.float32)
+    rank = jnp.where(owned, before.astype(jnp.int32), -1)
+    gate = jnp.sum(jnp.where(named, gates.astype(jnp.float32), 0.0), axis=2)
+    select = rank[:, None, :] == jnp.arange(most, dtype=jnp.int32)[None, :, None]
+    rows = lax.dot_general(
+        select.astype(jnp.bfloat16), grads, (((2,), (1,)), ((0,), (0,))), preferred_element_type=jnp.bfloat16
+    )
+    back = project_back(rows, down_weight[0, 0]).reshape(experts, most, hidden_width)
+    weight = jnp.sum(jnp.where(select, gate[:, None, :], 0.0), axis=2)
+    hidden_grad = (weight[:, :, None] * back).astype(jnp.bfloat16)
+    slot_grad = jnp.sum(hidden_saved[0, 0].astype(jnp.float32) * back, axis=2)
+    by_token = jnp.sum(jnp.where(select, slot_grad[:, :, None], 0.0), axis=1)
+    returned = lax.all_to_all(by_token, "expert", split_axis=0, concat_axis=0, tiled=True)
+    mine = expert_ids[0][:, :, None] == jnp.arange(experts, dtype=jnp.int32)
+    gate_grad = jnp.sum(jnp.where(mine, returned.T[:, None, :], 0.0), axis=2)
+    return hidden_grad[None, None], gate_grad[None]
+
+
 def solution(mesh):
     in_specs = (
         P("section", "expert", None),
@@ -76,4 +109,4 @@
         P("section", "expert", None, None, None),
     )
     out_specs = (P("section", "expert", None, None, None), P("section", "expert", None))
-    return jax.shard_map(local, mesh=mesh, in_specs=in_specs, out_specs=out_specs, check_vma=False)
+    return jax.shard_map(gathered, mesh=mesh, in_specs=in_specs, out_specs=out_specs, check_vma=False)

time: 302 us -> 226 us (0.75); the launches traced: 298 us -> 226 us
  blocking collectives: 0 us -> 80.4 us
  local copies, waits for them, and re-layouts: 61.3 us -> 0.93 us
  starting transfers between devices: 59.1 us -> 4.36 us
  waiting for transfers between devices: 148 us -> 101 us
  between operations: 1.02 us -> 14 us
    all_to_all x4 -> x1, waiting for transfers between devices: 146 us -> 2.93 us  [gathered(): lax.all_to_all(by_token, 'expert', split_axis=0, concat_axis=0, tiled=True)]
    all_gather x0 -> x1, waiting for transfers between devices: none -> 95.8 us  [gathered(): grads = lax.all_gather(incoming, 'expert', axis=0)]
    all_gather x0 -> x2, blocking collectives: none -> 80.4 us  [the longest x1 43.2 us: gathered(): gates = lax.all_gather(gate_weights[0], 'expert', axis=0)]
    all_to_all x4 -> x1, starting transfers between devices: 58.5 us -> 3.8 us  [gathered(): lax.all_to_all(by_token, 'expert', split_axis=0, concat_axis=0, tiled=True)]
    scatter x3 -> x0, local copies, waits for them, and re-layouts: 48.8 us -> none  [the longest x2 41.2 us: pack_rows(): rows = jnp.zeros((experts * most, grad_local.shape[1]), jnp.bfloat16).at[...]
    gather x1 -> x0, local copies, waits for them, and re-layouts: 6.15 us -> none  [local(): returned.reshape(-1)[dest].reshape(1, expert_ids.shape[1], top_count)]
    another operation x3 -> x0, other arithmetic: 4.64 us -> none
    broadcast_in_dim x0 -> x1, other arithmetic: none -> 4.33 us  [gathered(): return (hidden_grad[None, None], gate_grad[None])]
  transfers between devices with their start and end apart: 6 -> 3, of which waited for: 4 -> 3; matrix products, arithmetic and copies ran while one was open for 23% -> 2% of each run, Pallas kernels for 0% -> 0%
where the time goes in v1:
time: 226 us
  waiting for transfers between devices  101 us (45%)
  blocking collectives  80.4 us (36%)
  matrix products  19.6 us (9%)
  between operations  14 us (6%)
  other arithmetic  5.87 us (3%)
  starting transfers between devices  4.36 us (2%)
    all_gather x1, waiting for transfers between devices, gathered(): grads = lax.all_gather(incoming, 'expert', axis=0)  95.8 us
    all_gather x1, blocking collectives, gathered(): gates = lax.all_gather(gate_weights[0], 'expert', axis=0)  43.2 us
    all_gather x1, blocking collectives, gathered(): ids = lax.all_gather(expert_ids[0], 'expert', axis=0)  37.2 us
    dot_general x1, matrix products, project_back(): lax.dot_general(flat_rows, weight_part, (((1,), (1,)), ((), ())), preferr...  19.4 us
  transfers between devices with their start and end apart: 3, of which 3 were waited for; matrix products, arithmetic and copies ran while one was open for 2% of the time, Pallas kernels for 0%

profile of v1, /device:TPU:0, one launch (start us, length us, event | category | flops | bytes accessed | tf_op | source)
XLA Modules:
  0.0 226.2 jit_solution(17874956408639091450)
XLA Ops:
  7.2 0.0 all-gather.3.cloned.1.call-start
  7.2 0.5 collective-permute-start
  7.7 2.3 %collective-permute-done = bf16[128,3584]{1,0:T(8,128)(2,1)S(1)} collective-permute-done((bf16[128,3584]{1,0:T(8,128)(2,1)}, bf16[128,3584]{1,0:T(8,128)(2,1)S(1)}, u32[]{:S(2)}, u32[]{:S(2)}) %collective-permute-start) | collective-permute-done | bytes 917536 | tf_op jit(solution)/shard_map/ppermute | solution.py:9
  10.0 0.0 copy-start
  10.0 0.9 copy-done
  11.0 0.0 all-gather.3.cloned.1.call-update
  11.0 43.2 %all_gather.13 = bf16[16,128,8]{1,2,0:T(8,128)(2,1)S(1)} all-gather(bf16[1,128,8]{1,2,0:T(8,128)(2,1)} %param.7), channel_id=1, replica_groups=mesh['section'=2,'expert'=16] {'expert'}, dimensions={0}, use_global_device_ids=true | all-gather | bytes 34816 | tf_op jit(solution)/shard_map/all_gather | solution.py:78
  54.2 37.2 %all_gather.12 = s32[16,128,8]{1,2,0:T(8,128)S(1)} all-gather(s32[1,128,8]{1,2,0:T(8,128)} %param.6), channel_id=1, replica_groups=mesh['section'=2,'expert'=16] {'expert'}, dimensions={0}, use_global_device_ids=true | all-gather | bytes 69632 | tf_op jit(solution)/shard_map/all_gather | solution.py:77
  91.4 0.1 fusion.6
  91.6 95.8 %all-gather.3.cloned.1.call-done = bf16[2048,3584]{1,0:T(8,128)(2,1)} async-done(((bf16[128,3584]{1,0:T(8,128)(2,1)}), bf16[2048,3584]{1,0:T(8,128)(2,1)}) %all-gather.3.cloned.1.call-update) | async-done | bytes 14680080 | tf_op jit(solution)/shard_map/all_gather | solution.py:80
  187.4 19.4 %fusion.4 = (f32[16,80]{1,0:T(8,128)S(1)}, f32[16,80,1024]{2,1,0:T(8,128)}) fusion(bf16[1,1,16,80,1024]{4,3,2,1,0:T(8,128)(2,1)} %param.9, bf16[1,1,1024,3584]{3,2,1,0:T(8,128)(2,1)} %param.8, bf16[16,128,3584]{2,1,0:T(8,128)(2,1)} %bitcast.27, s32[16,128]{1,0:T(8,128)S(1)} %fusion.6), kind=kOutput, calls=%fused_computation.4 | convolution fusion | flops 10573741056 | bytes 29897728 | tf_op jit(solution)/shard_map/dot_general | solution.py:36
  206.8 0.0 copy-start.1
  206.8 0.9 select_reduce_fusion
  207.7 3.8 %all-to-all-start = ((f32[16,1,128]{2,1,0:T(1,128)}), f32[16,1,128]{2,1,0:T(1,128)S(1)}, u32[]{:S(2)}, u32[]{:S(2)}) async-start(f32[16,1,128]{2,1,0:T(1,128)} %bitcast.8), calls=%async_computation | async-start | bytes 16384 | tf_op jit(solution)/shard_map/all_to_all | solution.py:97
  211.5 4.3 %fusion.5 = bf16[1,1,16,80,1024]{4,3,2,1,0:T(8,128)(2,1)} fusion(f32[16,80,1024]{2,1,0:T(8,128)} %get-tuple-element.7, f32[16,80]{1,0:T(8,128)S(1)} %get-tuple-element.3), kind=kLoop, calls=%fused_computation.6 | loop fusion | flops 2621440 | bytes 7869440 | tf_op jit(solution)/shard_map/broadcast_in_dim | solution.py:100
  215.8 2.9 %all-to-all-done = f32[16,1,128]{2,1,0:T(1,128)S(1)} async-done(((f32[16,1,128]{2,1,0:T(1,128)}), f32[16,1,128]{2,1,0:T(1,128)S(1)}, u32[]{:S(2)}, u32[]{:S(2)}) %all-to-all-start) | async-done | bytes 8224 | tf_op jit(solution)/shard_map/all_to_all | solution.py:97
  218.8 0.0 copy-done.1
  218.8 0.6 select_reduce_fusion.2
  (2 shorter events, 0.1 us)
Async XLA Ops:
  7.2 180.2 %all-gather.3.cloned.1.call-start = ((), (), s32[]{:S(2)}) async-start(), calls=%async_computation.1 | async-start | bytes 15597568 | tf_op jit(solution)/shard_map/all_gather | solution.py:80
  7.2 2.8 %collective-permute-start = (bf16[128,3584]{1,0:T(8,128)(2,1)}, bf16[128,3584]{1,0:T(8,128)(2,1)S(1)}, u32[]{:S(2)}, u32[]{:S(2)}) collective-permute-start(bf16[128,3584]{1,0:T(8,128)(2,1)} %bitcast.28), channel_id=1, source_target_pairs={{0,16},{16,0},{1,17},{17,1},{2,18},{18,2},{3,19},{19,3},{4,20},{20... | collective-permute-start | bytes 2752520 | tf_op jit(solution)/shard_map/ppermute | solution.py:9
  10.0 0.9 copy-start
  206.8 11.9 %copy-start.1 = (s32[1,128,8]{1,2,0:T(8,128)S(1)}, s32[1,128,8]{1,2,0:T(8,128)}, u32[]{:S(2)}) copy-start(s32[1,128,8]{1,2,0:T(8,128)} %param.6) | copy-start | bytes 12292
  207.7 11.1 %all-to-all-start = ((f32[16,1,128]{2,1,0:T(1,128)}), f32[16,1,128]{2,1,0:T(1,128)S(1)}, u32[]{:S(2)}, u32[]{:S(2)}) async-start(f32[16,1,128]{2,1,0:T(1,128)} %bitcast.8), calls=%async_computation | async-start | bytes 16384 | tf_op jit(solution)/shard_map/all_to_all | solution.py:97
Sparse Core Ops, SparseCore 0:
  11.3 176.0 all-gather.2

commit v2 on v1

v2 whole, which is shorter than its diff:
```python
import functools

import jax
import jax.numpy as jnp
from jax import lax
from jax.experimental import pallas as pl
from jax.experimental.pallas import tpu as pltpu
from jax.sharding import PartitionSpec as P

MESH = pl.DeviceIdType.MESH
DEPTH, BATCH = 4, 4


def shifted(x, axis, by):
    size = lax.axis_size(axis)
    return lax.ppermute(x, axis, [(i, (i + by) % size) for i in range(size)])


def project_back(rows_in, weight_part):
    flat_rows = rows_in.reshape(-1, rows_in.shape[2])
    return lax.dot_general(
        flat_rows, weight_part, (((1,), (1,)), ((), ())), preferred_element_type=jnp.float32
    )


def gathered(grad_out, expert_ids, gate_weights, down_weight, hidden_saved):
    experts = lax.axis_size("expert")
    most = hidden_saved.shape[3]
    width = grad_out.shape[2]
    tokens = grad_out.shape[1]
    hidden_width = down_weight.shape[2]
    me = lax.axis_index("expert")
    ids = lax.all_gather(expert_ids[0], "expert", axis=0)
    gates = lax.all_gather(gate_weights[0], "expert", axis=0)
    incoming = shifted(grad_out[0], "section", -1)
    grads = lax.all_gather(incoming, "expert", axis=0)
    named = ids == me
    owned = jnp.any(named, axis=2)
    place = jnp.arange(tokens, dtype=jnp.int32)
    earlier = (place[:, None] < place[None, :]).astype(jnp.bfloat16)
    before = jnp.dot(owned.astype(jnp.bfloat16), earlier, preferred_element_type=jnp.float32)
    rank = jnp.where(owned, before.astype(jnp.int32), -1)
    gate = jnp.sum(jnp.where(named, gates.astype(jnp.float32), 0.0), axis=2)
    select = rank[:, None, :] == jnp.arange(most, dtype=jnp.int32)[None, :, None]
    rows = lax.dot_general(
        select.astype(jnp.bfloat16), grads, (((2,), (1,)), ((0,), (0,))), preferred_element_type=jnp.bfloat16
    )
    back = project_back(rows, down_weight[0, 0]).reshape(experts, most, hidden_width)
    weight = jnp.sum(jnp.where(select, gate[:, None, :], 0.0), axis=2)
    hidden_grad = (weight[:, :, None] * back).astype(jnp.bfloat16)
    slot_grad = jnp.sum(hidden_saved[0, 0].astype(jnp.float32) * back, axis=2)
    by_token = jnp.sum(jnp.where(select, slot_grad[:, :, None], 0.0), axis=1)
    returned = lax.all_to_all(by_token, "expert", split_axis=0, concat_axis=0, tiled=True)
    mine = expert_ids[0][:, :, None] == jnp.arange(experts, dtype=jnp.int32)
    gate_grad = jnp.sum(jnp.where(mine, returned.T[:, None, :], 0.0), axis=2)
    return hidden_grad[None, None], gate_grad[None]


def column_parts(width):
    tiles = width // 128
    few = tiles * 3 // 28
    many = (tiles - 2 * few) // 2
    sizes = (many, tiles - 2 * few - many, few, few)
    parts, at = [], 0
    for order, size in zip(("zxy", "zyx", "xyz", "yxz"), sizes):
        if size:
            parts.append((order, at * 128, size * 128))
        at += size
    return parts


def relay_kernel(
    most, parts, grad_ref, meta_ref, down_hbm, saved_hbm, hidden_out, gate_out,
    tok, meta_all, down, saved, hidden, rows, back, sent_back, came_back,
    swap_sems, send_sems, recv_sems, meta_send, meta_recv, back_send, back_recv, local_sems,
):
    experts, tokens, width = tok.shape
    top = meta_ref.shape[0] // 2
    hidden_width = down.shape[0]
    section, me = lax.axis_index("section"), lax.axis_index("expert")
    other = 1 - section
    vz, vy, vx = me // 4, (me // 2) % 2, me % 2

    def at(z, y, x):
        return z * 4 + y * 2 + x

    x_peer, y_peer = at(vz, vy, 1 - vx), at(vz, 1 - vy, vx)

    load_down = pltpu.make_async_copy(down_hbm, down, local_sems.at[0])
    load_saved = pltpu.make_async_copy(saved_hbm, saved, local_sems.at[1])
    load_down.start()
    load_saved.start()

    barrier = pltpu.get_barrier_semaphore()

    def greet(sec, exp):
        pl.semaphore_signal(barrier, inc=1, device_id=(sec, exp), device_id_type=MESH)

    greet(other, me)
    greet(other, x_peer)
    greet(other, y_peer)
    pl.when(vz < DEPTH - 1)(lambda: greet(other, me + 4))
    pl.when(vz > 0)(lambda: greet(other, me - 4))

    @pl.loop(1, experts)
    def _(j):
        greet(section, (me + j) % experts)

    inner = (vz + 2) // 3 - vz // 3
    pl.semaphore_wait(barrier, experts + 3 + inner)

    half = vz // 2
    near = vz + half * (3 - 2 * vz)

    def block_of(k, dx, dy):
        z = (near, 1 - near, 2, 3)[k]
        z = z + half * (3 - 2 * z)
        return z, at(z, vy + dy * (1 - 2 * vy), vx + dx * (1 - 2 * vx))

    def hop(p, item, way, block, sec, peer, src):
        _, lo, size = parts[p]
        return pltpu.make_async_remote_copy(
            src_ref=src.at[:, pl.ds(lo, size)],
            dst_ref=tok.at[block, :, pl.ds(lo, size)],
            send_sem=send_sems.at[(p * experts + item) * 4 + way],
            recv_sem=recv_sems.at[p * experts + block],
            device_id=(sec, peer),
            device_id_type=MESH,
        )

    def hops(p, item, k, dx, dy, act):
        order = parts[p][0]
        z, block = block_of(k, dx, dy)
        own = k == 0 and dx == 0 and dy == 0
        src, sec = (grad_ref, other) if own else (tok.at[block], section)
        moved = {"x": dx, "y": dy, "z": k}
        for place, way in enumerate(order):
            if any(moved[d] for d in order[place + 1:]):
                continue
            if way == "x" and not dx:
                act(hop(p, item, 0, block, sec, x_peer, src))
            if way == "y" and not dy:
                act(hop(p, item, 1, block, sec, y_peer, src))
            if way == "z":
                pl.when(jnp.logical_and(vz < DEPTH - 1, z <= vz))(
                    lambda: act(hop(p, item, 2, block, sec, me + 4, src))
                )
                pl.when(jnp.logical_and(vz > 0, z >= vz))(
                    lambda: act(hop(p, item, 3, block, sec, me - 4, src))
                )

    items = sorted(
        ((k, dx, dy) for k in range(DEPTH) for dx in range(2) for dy in range(2)),
        key=lambda it: (sum(it), -it[0]),
    )

    def meta_copy(j):
        peer = (me + j) % experts
        return pltpu.make_async_remote_copy(
            src_ref=meta_ref, dst_ref=meta_all.at[me], send_sem=meta_send.at[j],
            recv_sem=meta_recv.at[me], device_id=(section, peer), device_id_type=MESH,
        )

    def meta_arrival(j):
        peer = (me + j) % experts
        return pltpu.make_async_remote_copy(
            src_ref=meta_ref, dst_ref=meta_all.at[peer], send_sem=meta_send.at[j],
            recv_sem=meta_recv.at[peer], device_id=(section, peer), device_id_type=MESH,
        )

    def swap_copy():
        return pltpu.make_async_remote_copy(
            src_ref=grad_ref, dst_ref=tok.at[me], send_sem=swap_sems.at[0],
            recv_sem=swap_sems.at[1], device_id=(other, me), device_id_type=MESH,
        )

    def back_copy(item, block):
        return pltpu.make_async_remote_copy(
            src_ref=sent_back.at[block], dst_ref=came_back.at[me], send_sem=back_send.at[item],
            recv_sem=back_recv.at[me], device_id=(section, block), device_id_type=MESH,
        )

    def back_arrival(item, block):
        return pltpu.make_async_remote_copy(
            src_ref=sent_back.at[block], dst_ref=came_back.at[block], send_sem=back_send.at[item],
            recv_sem=back_recv.at[block], device_id=(section, block), device_id_type=MESH,
        )

    start = lambda copy: copy.start()
    for p in range(len(parts)):
        hops(p, 0, 0, 0, 0, start)
    swap_copy().start()

    @pl.loop(1, experts)
    def _(j):
        meta_copy(j).start()

    meta_all[me] = meta_ref[...]

    def take(item):
        k, dx, dy = items[item]
        _, block = block_of(k, dx, dy)
        for p in range(len(parts)):
            hop(p, item, 0, block, section, x_peer, tok.at[block]).wait_recv()
            hops(p, item, k, dx, dy, start)

    iota = lambda shape, dim: lax.broadcasted_iota(jnp.int32, shape, dim).astype(jnp.float32)

    def owners(block):
        ids = meta_all[block, pl.ds(0, top), :]
        gates = meta_all[block, pl.ds(top, top), :]
        named = ids == me.astype(jnp.float32)
        owned = jnp.sum(jnp.where(named, 1.0, 0.0), axis=0, keepdims=True)
        gate = jnp.sum(jnp.where(named, gates, 0.0), axis=0, keepdims=True)
        earlier = jnp.where(iota((tokens, tokens), 0) < iota((tokens, tokens), 1), 1.0, 0.0)
        before = jnp.dot(
            jnp.broadcast_to(owned, (16, tokens)).astype(jnp.bfloat16),
            earlier.astype(jnp.bfloat16),
            preferred_element_type=jnp.float32,
        )[:1]
        rank = jnp.where(owned > 0.5, before, -1.0)
        return iota((most, tokens), 0) == rank, gate

    def work(first):
        blocks = [block_of(*items[first + i])[1] for i in range(BATCH)]
        for i, block in enumerate(blocks):
            select, _ = owners(block)
            rows[pl.ds(i * most, most), :] = jnp.dot(
                jnp.where(select, 1.0, 0.0).astype(jnp.bfloat16), tok[block],
                preferred_element_type=jnp.float32,
            ).astype(jnp.bfloat16)

        @pl.loop(0, hidden_width // 256)
        def _(j):
            at_j = pl.ds(pl.multiple_of(j * 256, 256), 256)
            back[:, at_j] = lax.dot_general(
                rows[...], down[at_j, :], (((1,), (1,)), ((), ())),
                preferred_element_type=jnp.float32,
            )

        for i, block in enumerate(blocks):
            select, gate = owners(block)
            weight = jnp.sum(jnp.where(select, gate, 0.0), axis=1, keepdims=True)
            value = back[pl.ds(i * most, most), :]
            hidden[block] = (weight * value).astype(jnp.bfloat16)
            slot = jnp.sum(saved[block].astype(jnp.float32) * value, axis=1, keepdims=True)
            by_token = jnp.sum(jnp.where(select, slot, 0.0), axis=0, keepdims=True)
            by_token = jnp.broadcast_to(by_token, (8, tokens))
            if first + i == 0:
                came_back[block] = by_token
            else:
                sent_back[block] = by_token
                back_copy(first + i, block).start()
            hidden_store(first + i, block).start()

    def hidden_store(item, block):
        return pltpu.make_async_copy(hidden.at[block], hidden_out.at[block], local_sems.at[2 + item])

    for item in range(1, 8):
        take(item)

    @pl.loop(1, experts)
    def _(j):
        meta_arrival(j).wait_recv()

    swap_copy().wait_recv()
    load_down.wait()
    load_saved.wait()
    work(0)
    for item in range(8, 12):
        take(item)
    work(4)
    for item in range(12, 15):
        take(item)
    work(8)
    take(15)
    work(12)

    for item, (k, dx, dy) in enumerate(items):
        block = block_of(k, dx, dy)[1]
        hidden_store(item, block).wait()
        for p in range(len(parts)):
            hops(p, item, k, dx, dy, lambda copy: copy.wait_send())
    swap_copy().wait_send()

    @pl.loop(1, experts)
    def _(j):
        meta_copy(j).wait_send()

    for item in range(1, experts):
        block = block_of(*items[item])[1]
        back_arrival(item, block).wait_recv()
        back_copy(item, block).wait_send()
    ids = meta_ref[pl.ds(0, top), :]
    total = jnp.zeros((top, tokens), jnp.float32)
    for e in range(experts):
        total += jnp.where(ids == float(e), came_back[e], 0.0)
    gate_out[...] = total


def relayed(grad_out, expert_ids, gate_weights, down_weight, hidden_saved):
    experts = lax.axis_size("expert")
    tokens, width = grad_out.shape[1:]
    most, hidden_width = hidden_saved.shape[3:]
    top = expert_ids.shape[2]
    meta = jnp.concatenate(
        [expert_ids[0].T.astype(jnp.float32), gate_weights[0].T.astype(jnp.float32)], axis=0
    )
    parts = column_parts(width)
    f32, bf16 = jnp.float32, jnp.bfloat16
    dma = pltpu.SemaphoreType.DMA
    vmem, any_space = pl.BlockSpec(memory_space=pltpu.VMEM), pl.BlockSpec(memory_space=pl.ANY)
    hidden_grad, gate_rows = pl.pallas_call(
        functools.partial(relay_kernel, most, parts),
        out_shape=(
            jax.ShapeDtypeStruct((experts, most, hidden_width), bf16),
            jax.ShapeDtypeStruct((top, tokens), f32),
        ),
        in_specs=[vmem, vmem, any_space, any_space],
        out_specs=(any_space, vmem),
        scratch_shapes=[
            pltpu.VMEM((experts, tokens, width), bf16),
            pltpu.VMEM((experts, 2 * top, tokens), f32),
            pltpu.VMEM((hidden_width, width), bf16),
            pltpu.VMEM((experts, most, hidden_width), bf16),
            pltpu.VMEM((experts, most, hidden_width), bf16),
            pltpu.VMEM((BATCH * most, width), bf16),
            pltpu.VMEM((BATCH * most, hidden_width), f32),
            pltpu.VMEM((experts, 8, tokens), f32),
            pltpu.VMEM((experts, 8, tokens), f32),
            dma((2,)),
            dma((len(parts) * experts * 4,)),
            dma((len(parts) * experts,)),
            dma((experts,)),
            dma((experts,)),
            dma((experts,)),
            dma((experts,)),
            dma((2 + experts,)),
        ],
        compiler_params=pltpu.CompilerParams(
            collective_id=0, has_side_effects=True, vmem_limit_bytes=56 * 1024 * 1024
        ),
        cost_estimate=pl.CostEstimate(
            flops=2 * experts * most * width * hidden_width, bytes_accessed=16 * 1024 * 1024, transcendentals=0
        ),
    )(grad_out[0], meta, down_weight[0, 0], hidden_saved[0, 0])
    return hidden_grad[None, None], gate_rows.T[None]


def fits_relay(mesh):
    return mesh.shape["section"] == 2 and mesh.shape["expert"] == DEPTH * 4


def solution(mesh):
    in_specs = (
        P("section", "expert", None),
        P("section", "expert", None),
        P("section", "expert", None),
        P("section", "expert", None, None),
        P("section", "expert", None, None, None),
    )
    out_specs = (P("section", "expert", None, None, None), P("section", "expert", None))
    local_step = relayed if fits_relay(mesh) else gathered
    return jax.shard_map(local_step, mesh=mesh, in_specs=in_specs, out_specs=out_specs, check_vma=False)
```

time: 226 us -> 135 us (0.60)
  Pallas kernels: 0 us -> 128 us
  waiting for transfers between devices: 101 us -> 0 us
  blocking collectives: 80.4 us -> 0 us
  matrix products: 19.6 us -> 0 us
  between operations: 14 us -> 0.65 us
  starting transfers between devices: 4.36 us -> 0 us
  other arithmetic: 5.87 us -> 1.97 us
  local copies, waits for them, and re-layouts: 0.93 us -> 4.15 us
    pallas_call x0 -> x1, Pallas kernels: none -> 128 us  [relayed(): pl.pallas_call(functools.partial(relay_kernel, most, parts), out_shape=(j...]
    all_gather x1 -> x0, waiting for transfers between devices: 95.8 us -> none  [gathered(): grads = lax.all_gather(incoming, 'expert', axis=0)]
    all_gather x2 -> x0, blocking collectives: 80.4 us -> none  [the longest x1 43.2 us: gathered(): gates = lax.all_gather(gate_weights[0], 'expert', axis=0)]
    dot_general x2 -> x0, matrix products: 19.6 us -> none  [the longest x1 19.4 us: project_back(): lax.dot_general(flat_rows, weight_part, (((1,), (1,)), ((), ())), preferr...]
    broadcast_in_dim x1 -> x0, other arithmetic: 4.33 us -> none  [gathered(): return (hidden_grad[None, None], gate_grad[None])]
    all_to_all x1 -> x0, starting transfers between devices: 3.8 us -> none  [gathered(): lax.all_to_all(by_token, 'expert', split_axis=0, concat_axis=0, tiled=True)]
    unnamed x4, local copies, waits for them, and re-layouts: 0.93 us -> 4.15 us
    all_to_all x1 -> x0, waiting for transfers between devices: 2.93 us -> none  [gathered(): lax.all_to_all(by_token, 'expert', split_axis=0, concat_axis=0, tiled=True)]
  transfers between devices with their start and end apart: 3 -> 0, of which waited for: 3 -> 0; matrix products, arithmetic and copies ran while one was open for 2% -> 0% of each run, Pallas kernels for 0% -> 0%
where the time goes in v2:
time: 135 us
  Pallas kernels  128 us (95%)
  local copies, waits for them, and re-layouts  4.15 us (3%)
  other arithmetic  1.97 us (1%)
    pallas_call x1, Pallas kernels, relayed(): pl.pallas_call(functools.partial(relay_kernel, most, parts), out_shape=(j...  128 us
    unnamed x4, local copies, waits for them, and re-layouts  4.15 us

profile of v2, /device:TPU:0, one launch (start us, length us, event | category | flops | bytes accessed | tf_op | source)
XLA Modules:
  0.0 134.7 jit_solution(9182901409215528209)
XLA Ops:
  0.6 0.7 convert_bitcast_fusion.1
  1.3 0.7 convert_bitcast_fusion
  2.0 0.6 pad_maximum_fusion.meta_ref
  2.6 128.0 %shard_map.68 = (bf16[16,80,1024]{2,1,0:T(8,128)(2,1)}, f32[8,128]{1,0:T(8,128)}) custom-call(bf16[128,3584]{1,0:T(8,128)(2,1)} %bitcast.20, f32[16,128]{1,0:T(8,128)} %pad_maximum_fusion.meta_ref, bf16[1024,3584]{1,0:T(8,128)(2,1)} %bitcast.18, bf16[16,80,1024]{2,1,0:T(8,128)(2,1)} %bitcast.19), custom_call_target="tpu_custom_call" | custom-call | flops 9395240960 | bytes 16777216 | tf_op jit(solution)/shard_map/pallas_call | solution.py:313
  130.6 0.0 copy-start
  130.6 3.6 %copy.9 = bf16[1,1,16,80,1024]{4,3,2,1,0:T(8,128)(2,1)} copy(bf16[1,1,16,80,1024]{4,3,2,1,0:T(8,128)(2,1)} %bitcast.16) | data formatting | bytes 5242880
  134.1 0.0 copy-done
  134.1 0.6 copy.10
Async XLA Ops:
  130.6 3.6 %copy-start = (f32[8,128]{1,0:T(8,128)S(1)}, f32[8,128]{1,0:T(8,128)}, u32[]{:S(2)}) copy-start(f32[8,128]{1,0:T(8,128)} %get-tuple-element.5) | copy-start | bytes 12292

commit v3 on v2

--- a/solution.py
+++ b/solution.py
@@ -58,7 +58,7 @@
 
 def column_parts(width):
     tiles = width // 128
-    few = tiles * 3 // 28
+    few = tiles * 1 // 28
     many = (tiles - 2 * few) // 2
     sizes = (many, tiles - 2 * few - many, few, few)
     parts, at = [], 0
@@ -70,8 +70,8 @@
 
 
 def relay_kernel(
-    most, parts, grad_ref, meta_ref, down_hbm, saved_hbm, hidden_out, gate_out,
-    tok, meta_all, down, saved, hidden, rows, back, sent_back, came_back,
+    most, parts, grad_ref, ids_ref, gates_ref, down_hbm, saved_hbm, hidden_out, gate_out,
+    tok, meta_ref, meta_all, meta_other, ranks, down, saved, hidden, rows, packed, back, sent_back, came_back,
     swap_sems, send_sems, recv_sems, meta_send, meta_recv, back_send, back_recv, local_sems,
 ):
     experts, tokens, width = tok.shape
@@ -85,6 +85,7 @@
         return z * 4 + y * 2 + x
 
     x_peer, y_peer = at(vz, vy, 1 - vx), at(vz, 1 - vy, vx)
+    iota = lambda shape, dim: lax.broadcasted_iota(jnp.int32, shape, dim).astype(jnp.float32)
 
     load_down = pltpu.make_async_copy(down_hbm, down, local_sems.at[0])
     load_saved = pltpu.make_async_copy(saved_hbm, saved, local_sems.at[1])
@@ -127,6 +128,50 @@
             device_id=(sec, peer),
             device_id_type=MESH,
         )
+
+    items = sorted(
+        ((k, dx, dy) for k in range(DEPTH) for dx in range(2) for dy in range(2)),
+        key=lambda it: (sum(it), -it[0]),
+    )
+
+    def is_packed(p, item):
+        return parts[p][0][0] == "z" and bool(items[item]["zxy".index(parts[p][0][2])])
+
+    def packed_hop(p, item, way):
+        order, lo, size = parts[p]
+        k, dx, dy = items[item]
+        block = block_of(k, dx, dy)[1]
+        there = items.index((k, 1, dy) if way == 0 else (k, dx, 1))
+        slot = [it for it in items if not it["zxy".index(order[2])]].index((k, dx, dy))
+        return slot, pltpu.make_async_remote_copy(
+            src_ref=packed.at[p, slot, :, pl.ds(0, size)],
+            dst_ref=rows.at[there, :, pl.ds(lo, size)],
+            send_sem=send_sems.at[(p * experts + item) * 4 + way],
+            recv_sem=recv_sems.at[p * experts + block],
+            device_id=(other if item == 0 else section, x_peer if way == 0 else y_peer),
+            device_id_type=MESH,
+        )
+
+    def packed_way(p, item):
+        order = parts[p][0]
+        if order[0] != "z" or is_packed(p, item):
+            return None
+        return "xy".index(order[2])
+
+    def pack_and_send(p, item, rank):
+        way = packed_way(p, item)
+        slot, copy = packed_hop(p, item, way)
+        _, lo, size = parts[p]
+        block = block_of(*items[item])[1]
+        source = grad_ref[:, pl.ds(lo, size)] if item == 0 else tok[block, :, pl.ds(lo, size)]
+        packed[p, slot, :, pl.ds(0, size)] = chosen(rank, source)
+        copy.start()
+
+    def chosen(rank, source):
+        select = iota((most, tokens), 0) == rank
+        return jnp.dot(
+            jnp.where(select, 1.0, 0.0).astype(jnp.bfloat16), source, preferred_element_type=jnp.float32
+        ).astype(jnp.bfloat16)
 
     def hops(p, item, k, dx, dy, act):
         order = parts[p][0]
@@ -136,6 +181,8 @@
         moved = {"x": dx, "y": dy, "z": k}
         for place, way in enumerate(order):
             if any(moved[d] for d in order[place + 1:]):
+                continue
+            if order[0] == "z" and place == 2:
                 continue
             if way == "x" and not dx:
                 act(hop(p, item, 0, block, sec, x_peer, src))
@@ -149,11 +196,6 @@
                     lambda: act(hop(p, item, 3, block, sec, me - 4, src))
                 )
 
-    items = sorted(
-        ((k, dx, dy) for k in range(DEPTH) for dx in range(2) for dy in range(2)),
-        key=lambda it: (sum(it), -it[0]),
-    )
-
     def meta_copy(j):
         peer = (me + j) % experts
         return pltpu.make_async_remote_copy(
@@ -172,6 +214,12 @@
         return pltpu.make_async_remote_copy(
             src_ref=grad_ref, dst_ref=tok.at[me], send_sem=swap_sems.at[0],
             recv_sem=swap_sems.at[1], device_id=(other, me), device_id_type=MESH,
+        )
+
+    def meta_swap():
+        return pltpu.make_async_remote_copy(
+            src_ref=meta_ref, dst_ref=meta_other, send_sem=swap_sems.at[2],
+            recv_sem=swap_sems.at[3], device_id=(other, me), device_id_type=MESH,
         )
 
     def back_copy(item, block):
@@ -189,57 +237,94 @@
     start = lambda copy: copy.start()
     for p in range(len(parts)):
         hops(p, 0, 0, 0, 0, start)
-    swap_copy().start()
+    meta_ref[pl.ds(0, top), :] = ids_ref[...].astype(jnp.float32)
+    meta_ref[pl.ds(top, top), :] = gates_ref[...].astype(jnp.float32)
+    meta_swap().start()
 
     @pl.loop(1, experts)
     def _(j):
         meta_copy(j).start()
 
     meta_all[me] = meta_ref[...]
+    swap_copy().start()
+
+    def owned_by(ids, expert):
+        return jnp.max(jnp.where(ids == expert.astype(jnp.float32), 1.0, 0.0), axis=0, keepdims=True)
+
+    def ranks_of(owned):
+        earlier = jnp.where(iota((tokens, tokens), 0) < iota((tokens, tokens), 1), 1.0, 0.0)
+        before = jnp.dot(
+            owned.astype(jnp.bfloat16), earlier.astype(jnp.bfloat16), preferred_element_type=jnp.float32
+        )
+        return jnp.where(owned > 0.5, before, -1.0)
+
+    meta_swap().wait_recv()
+    ids = meta_other[pl.ds(0, top), :]
+    owned = [owned_by(ids, peer) for peer in (x_peer, y_peer)]
+    own_ranks = ranks_of(jnp.concatenate([owned[0]] * 8 + [owned[1]] * 8, axis=0))
+    for p in range(len(parts)):
+        way = packed_way(p, 0)
+        if way is not None:
+            pack_and_send(p, 0, own_ranks[8 * way:8 * way + 1])
+
+    @pl.loop(1, experts)
+    def _(j):
+        meta_arrival(j).wait_recv()
+
+    for i, expert in enumerate((x_peer, y_peer, me)):
+        table = jnp.concatenate(
+            [owned_by(meta_all[b, pl.ds(0, top), :], expert) for b in range(experts)], axis=0
+        )
+        table = ranks_of(table)
+        for b in range(experts):
+            ranks[i, b] = table[b:b + 1]
 
     def take(item):
         k, dx, dy = items[item]
         _, block = block_of(k, dx, dy)
         for p in range(len(parts)):
+            if is_packed(p, item):
+                continue
             hop(p, item, 0, block, section, x_peer, tok.at[block]).wait_recv()
             hops(p, item, k, dx, dy, start)
-
-    iota = lambda shape, dim: lax.broadcasted_iota(jnp.int32, shape, dim).astype(jnp.float32)
-
-    def owners(block):
-        ids = meta_all[block, pl.ds(0, top), :]
-        gates = meta_all[block, pl.ds(top, top), :]
-        named = ids == me.astype(jnp.float32)
-        owned = jnp.sum(jnp.where(named, 1.0, 0.0), axis=0, keepdims=True)
-        gate = jnp.sum(jnp.where(named, gates, 0.0), axis=0, keepdims=True)
-        earlier = jnp.where(iota((tokens, tokens), 0) < iota((tokens, tokens), 1), 1.0, 0.0)
-        before = jnp.dot(
-            jnp.broadcast_to(owned, (16, tokens)).astype(jnp.bfloat16),
-            earlier.astype(jnp.bfloat16),
-            preferred_element_type=jnp.float32,
-        )[:1]
-        rank = jnp.where(owned > 0.5, before, -1.0)
-        return iota((most, tokens), 0) == rank, gate
+            way = packed_way(p, item)
+            if way is not None:
+                pack_and_send(p, item, ranks[way, block])
+
+    def finish(item):
+        block = block_of(*items[item])[1]
+        rank = ranks[2, block]
+        for p, (_, lo, size) in enumerate(parts):
+            if is_packed(p, item):
+                pltpu.make_async_remote_copy(
+                    src_ref=rows.at[item, :, pl.ds(lo, size)],
+                    dst_ref=rows.at[item, :, pl.ds(lo, size)],
+                    send_sem=send_sems.at[0],
+                    recv_sem=recv_sems.at[p * experts + block],
+                    device_id=(section, x_peer),
+                    device_id_type=MESH,
+                ).wait_recv()
+            else:
+                rows[item, :, pl.ds(lo, size)] = chosen(rank, tok[block, :, pl.ds(lo, size)])
 
     def work(first):
         blocks = [block_of(*items[first + i])[1] for i in range(BATCH)]
-        for i, block in enumerate(blocks):
-            select, _ = owners(block)
-            rows[pl.ds(i * most, most), :] = jnp.dot(
-                jnp.where(select, 1.0, 0.0).astype(jnp.bfloat16), tok[block],
-                preferred_element_type=jnp.float32,
-            ).astype(jnp.bfloat16)
+        for i in range(BATCH):
+            finish(first + i)
 
         @pl.loop(0, hidden_width // 256)
         def _(j):
             at_j = pl.ds(pl.multiple_of(j * 256, 256), 256)
             back[:, at_j] = lax.dot_general(
-                rows[...], down[at_j, :], (((1,), (1,)), ((), ())),
+                rows[pl.ds(first, BATCH)].reshape(BATCH * most, width), down[at_j, :], (((1,), (1,)), ((), ())),
                 preferred_element_type=jnp.float32,
             )
 
         for i, block in enumerate(blocks):
-            select, gate = owners(block)
+            named = meta_all[block, pl.ds(0, top), :] == me.astype(jnp.float32)
+            gate = jnp.where(named, meta_all[block, pl.ds(top, top), :], 0.0)
+            gate = jnp.sum(gate, axis=0, keepdims=True)
+            select = iota((most, tokens), 0) == ranks[2, block]
             weight = jnp.sum(jnp.where(select, gate, 0.0), axis=1, keepdims=True)
             value = back[pl.ds(i * most, most), :]
             hidden[block] = (weight * value).astype(jnp.bfloat16)
@@ -259,10 +344,6 @@
     for item in range(1, 8):
         take(item)
 
-    @pl.loop(1, experts)
-    def _(j):
-        meta_arrival(j).wait_recv()
-
     swap_copy().wait_recv()
     load_down.wait()
     load_saved.wait()
@@ -281,7 +362,11 @@
         hidden_store(item, block).wait()
         for p in range(len(parts)):
             hops(p, item, k, dx, dy, lambda copy: copy.wait_send())
+            way = packed_way(p, item)
+            if way is not None:
+                packed_hop(p, item, way)[1].wait_send()
     swap_copy().wait_send()
+    meta_swap().wait_send()
 
     @pl.loop(1, experts)
     def _(j):
@@ -303,9 +388,6 @@
     tokens, width = grad_out.shape[1:]
     most, hidden_width = hidden_saved.shape[3:]
     top = expert_ids.shape[2]
-    meta = jnp.concatenate(
-        [expert_ids[0].T.astype(jnp.float32), gate_weights[0].T.astype(jnp.float32)], axis=0
-    )
     parts = column_parts(width)
     f32, bf16 = jnp.float32, jnp.bfloat16
     dma = pltpu.SemaphoreType.DMA
@@ -316,19 +398,23 @@
             jax.ShapeDtypeStruct((experts, most, hidden_width), bf16),
             jax.ShapeDtypeStruct((top, tokens), f32),
         ),
-        in_specs=[vmem, vmem, any_space, any_space],
+        in_specs=[vmem, vmem, vmem, any_space, any_space],
         out_specs=(any_space, vmem),
         scratch_shapes=[
             pltpu.VMEM((experts, tokens, width), bf16),
+            pltpu.VMEM((2 * top, tokens), f32),
             pltpu.VMEM((experts, 2 * top, tokens), f32),
+            pltpu.VMEM((2 * top, tokens), f32),
+            pltpu.VMEM((3, experts, 1, tokens), f32),
             pltpu.VMEM((hidden_width, width), bf16),
             pltpu.VMEM((experts, most, hidden_width), bf16),
             pltpu.VMEM((experts, most, hidden_width), bf16),
-            pltpu.VMEM((BATCH * most, width), bf16),
+            pltpu.VMEM((experts, most, width), bf16),
+            pltpu.VMEM((2, 8, most, max(size for _, _, size in parts)), bf16),
             pltpu.VMEM((BATCH * most, hidden_width), f32),
             pltpu.VMEM((experts, 8, tokens), f32),
             pltpu.VMEM((experts, 8, tokens), f32),
-            dma((2,)),
+            dma((4,)),
             dma((len(parts) * experts * 4,)),
             dma((len(parts) * experts,)),
             dma((experts,)),
@@ -343,7 +429,7 @@
         cost_estimate=pl.CostEstimate(
             flops=2 * experts * most * width * hidden_width, bytes_accessed=16 * 1024 * 1024, transcendentals=0
         ),
-    )(grad_out[0], meta, down_weight[0, 0], hidden_saved[0, 0])
+    )(grad_out[0], expert_ids[0].T, gate_weights[0].T, down_weight[0, 0], hidden_saved[0, 0])
     return hidden_grad[None, None], gate_rows.T[None]
 
 

time: 135 us -> 119 us (0.88)
  Pallas kernels: 128 us -> 114 us
  other arithmetic: 1.97 us -> 0 us
    pallas_call x1, Pallas kernels: 128 us -> 114 us  [relayed(): pl.pallas_call(functools.partial(relay_kernel, most, parts), out_shape=(j...]
    convert_element_type x2 -> x0, other arithmetic: 1.37 us -> none  [the longest x1 0.69 us: relayed(): expert_ids[0].T.astype(jnp.float32)]
where the time goes in v3:
time: 119 us
  Pallas kernels  114 us (96%)
  local copies, waits for them, and re-layouts  4.15 us (3%)
    pallas_call x1, Pallas kernels, relayed(): pl.pallas_call(functools.partial(relay_kernel, most, parts), out_shape=(j...  114 us
    unnamed x4, local copies, waits for them, and re-layouts  4.15 us

profile of v3, /device:TPU:0, one launch (start us, length us, event | category | flops | bytes accessed | tf_op | source)
XLA Modules:
  0.0 119.2 jit_solution(6919402757291853526)
XLA Ops:
  0.6 114.4 %shard_map.68 = (bf16[16,80,1024]{2,1,0:T(8,128)(2,1)}, f32[8,128]{1,0:T(8,128)}) custom-call(bf16[128,3584]{1,0:T(8,128)(2,1)} %bitcast.17, s32[8,128]{1,0:T(8,128)} %bitcast.18, bf16[8,128]{1,0:T(8,128)(2,1)} %bitcast.19, bf16[1024,3584]{1,0:T(8,128)(2,1)} %bitcast.15, bf16[16,80,1024]{2,1,0:T(8,128)(2,1)} %bitcast.16), custom_call_target="tpu_custom_call" | custom-call | flops 9395240960 | bytes 16777216 | tf_op jit(solution)/shard_map/pallas_call | solution.py:395
  115.1 0.0 copy-start
  115.1 3.6 %copy.9 = bf16[1,1,16,80,1024]{4,3,2,1,0:T(8,128)(2,1)} copy(bf16[1,1,16,80,1024]{4,3,2,1,0:T(8,128)(2,1)} %bitcast.13) | data formatting | bytes 5242880
  118.6 0.0 copy-done
  118.6 0.6 copy.10
Async XLA Ops:
  115.1 3.6 %copy-start = (f32[8,128]{1,0:T(8,128)S(1)}, f32[8,128]{1,0:T(8,128)}, u32[]{:S(2)}) copy-start(f32[8,128]{1,0:T(8,128)} %get-tuple-element.5) | copy-start | bytes 12292

commit v4 on v3

--- a/solution.py
+++ b/solution.py
@@ -312,9 +312,9 @@
         for i in range(BATCH):
             finish(first + i)
 
-        @pl.loop(0, hidden_width // 256)
+        @pl.loop(0, hidden_width // 512)
         def _(j):
-            at_j = pl.ds(pl.multiple_of(j * 256, 256), 256)
+            at_j = pl.ds(pl.multiple_of(j * 512, 512), 512)
             back[:, at_j] = lax.dot_general(
                 rows[pl.ds(first, BATCH)].reshape(BATCH * most, width), down[at_j, :], (((1,), (1,)), ((), ())),
                 preferred_element_type=jnp.float32,

time: 119 us -> 119 us (level)
  no operation moved by 1% of the time
where the time goes in v4:
time: 119 us
  Pallas kernels  114 us (96%)
  local copies, waits for them, and re-layouts  4.15 us (3%)
    pallas_call x1, Pallas kernels, relayed(): pl.pallas_call(functools.partial(relay_kernel, most, parts), out_shape=(j...  114 us
    unnamed x4, local copies, waits for them, and re-layouts  4.15 us

profile of v4, /device:TPU:0, one launch (start us, length us, event | category | flops | bytes accessed | tf_op | source)
XLA Modules:
  0.0 118.7 jit_solution(11163743035084243206)
XLA Ops:
  0.6 113.9 %shard_map.68 = (bf16[16,80,1024]{2,1,0:T(8,128)(2,1)}, f32[8,128]{1,0:T(8,128)}) custom-call(bf16[128,3584]{1,0:T(8,128)(2,1)} %bitcast.17, s32[8,128]{1,0:T(8,128)} %bitcast.18, bf16[8,128]{1,0:T(8,128)(2,1)} %bitcast.19, bf16[1024,3584]{1,0:T(8,128)(2,1)} %bitcast.15, bf16[16,80,1024]{2,1,0:T(8,128)(2,1)} %bitcast.16), custom_call_target="tpu_custom_call" | custom-call | flops 9395240960 | bytes 16777216 | tf_op jit(solution)/shard_map/pallas_call | solution.py:395
  114.5 0.0 copy-start
  114.5 3.6 %copy.9 = bf16[1,1,16,80,1024]{4,3,2,1,0:T(8,128)(2,1)} copy(bf16[1,1,16,80,1024]{4,3,2,1,0:T(8,128)(2,1)} %bitcast.13) | data formatting | bytes 5242880
  118.1 0.0 copy-done
  118.1 0.6 copy.10
Async XLA Ops:
  114.5 3.6 %copy-start = (f32[8,128]{1,0:T(8,128)S(1)}, f32[8,128]{1,0:T(8,128)}, u32[]{:S(2)}) copy-start(f32[8,128]{1,0:T(8,128)} %get-tuple-element.5) | copy-start | bytes 12292
